TPU v7x, 256 devices: a whole 4x4x8 slice. The times are simulated.
256 devices in a mesh: noise: 8 (over z), row: 16 (over y, x), col: 2 (over core).
Axes of the slice: x: 4, y: 4, z: 8, core: 2. Of those that a mesh axis runs over, the one named last changes fastest.
Arguments:
- images: bfloat16 [256, 4, 6144], P('row', None, 'col'), may hold values from -40 to 40
- gain: float32 [6144], P('col'), may hold values from 0.3 to 3.5
- up_weight: bfloat16 [6144, 12288], P('col', 'row'), may hold values from -0.078125 to 0.078125
- down_weight: bfloat16 [12288, 6144], P('row', 'col'), may hold values from -0.0546875 to 0.0546875
- cotangent: bfloat16 [256, 16, 6144], P('row', 'noise', 'col'), may hold values from -6 to 6
- seeds: int32 [16], P('noise'), may hold values from 0 to 999999
- assign: int32 [16, 1], replicated, may hold values from 0 to 3, as said below
Outputs:
- saliency: float32 [256, 4, 6144], P('row', None, 'col')
Inputs may be any that keep to these rules, and one draw needn't show every extreme that they name: `assign`: every one of the 4 images is named by at least one copy.
All inputs are finite; a program needn't handle non-finite values.
Results may differ from a plain program's by a relative error of at most 0.0019.
Values may be sent and summed in bfloat16 or wider, within the bound.
A program may use at most 64 MiB of HBM per device.

v0:
```python
import math
import jax
import jax.numpy as jnp
from jax import lax
from jax.sharding import PartitionSpec as P

D = 6144
noise_scale = 0.6
gelu_coef = 0.044715
root_term = math.sqrt(2.0 / math.pi)


def mix_noise(seed_value, token_index, feature_index, width):
    linear = token_index[:, None] * width + feature_index[None, :]
    mixed = linear * 1664525 + seed_value * 1013904223
    mixed = mixed ^ mixed >> 13
    mixed = mixed * 1274126177
    mixed = mixed ^ mixed >> 16
    return ((mixed & 65535).astype(jnp.float32) - 32767.5) * (1.0 / 18918.0)


def gelu_slope(preact):
    inner = root_term * (preact + gelu_coef * preact * preact * preact)
    tanh_val = jnp.tanh(inner)
    return 0.5 * (1.0 + tanh_val) + 0.5 * preact * (1.0 - tanh_val * tanh_val) * root_term * (
        1.0 + 3.0 * gelu_coef * preact * preact
    )


def body(images, gain, up_weight, down_weight, cotangent, seeds, assign):
    tok_local = images.shape[0]
    image_count = images.shape[1]
    width_local = images.shape[2]
    planes = lax.axis_size("noise")
    rows = lax.axis_size("row")
    part = tok_local // planes
    col_index = lax.axis_index("col")
    row_index = lax.axis_index("row")
    noise_index = lax.axis_index("noise")
    all_seeds = lax.all_gather(seeds, "noise", tiled=True)
    slots = all_seeds.shape[0]
    own_cot = lax.all_to_all(cotangent, "noise", split_axis=0, concat_axis=1, tiled=True)
    own_images = lax.dynamic_slice_in_dim(images, noise_index * part, part)
    plane_images = lax.all_gather(own_images, "row", axis=0, tiled=True)
    plane_cot = lax.all_gather(own_cot, "row", axis=0, tiled=True)
    image_ids = jnp.arange(image_count, dtype=jnp.int32)
    onehot = (assign[:, 0][:, None] == image_ids[None, :]).astype(jnp.float32)
    counts = jnp.sum(onehot, axis=0)
    clean = jnp.einsum(
        "si,tid->tsd", onehot.astype(jnp.bfloat16), plane_images, preferred_element_type=jnp.float32
    )
    tokens = (
        jnp.arange(rows, dtype=jnp.int32)[:, None] * tok_local
        + noise_index * part
        + jnp.arange(part, dtype=jnp.int32)[None, :]
    ).reshape(-1)
    feature_index = col_index * width_local + jnp.arange(width_local, dtype=jnp.int32)
    noise_field = jax.vmap(
        lambda seed_value: mix_noise(seed_value, tokens, feature_index, D), out_axes=1
    )(all_seeds)
    noisy = clean + noise_scale * noise_field
    feat_mean = lax.psum(jnp.sum(noisy, axis=-1), "col") / D
    centred = noisy - feat_mean[..., None]
    feat_var = lax.psum(jnp.sum(centred * centred, axis=-1), "col") / D
    inv_std = lax.rsqrt(feat_var + 1e-06)
    normed = centred * inv_std[..., None]
    scaled = (normed * gain).astype(jnp.bfloat16)
    n = tokens.shape[0] * slots
    preact_part = jnp.dot(
        scaled.reshape(n, width_local), up_weight, preferred_element_type=jnp.float32
    )
    back_part = jnp.einsum(
        "td,hd->th",
        plane_cot.reshape(n, width_local),
        down_weight,
        preferred_element_type=jnp.float32,
    )
    ug_part = jnp.sum(gain[:, None] * up_weight.astype(jnp.float32), axis=0)
    preact, back_grad, ug = lax.psum((preact_part, back_part, ug_part), "col")
    hidden_grad = (back_grad * gelu_slope(preact)).astype(jnp.bfloat16)
    hg = hidden_grad.astype(jnp.float32)
    sums = jnp.stack([jnp.sum(hg * ug, axis=-1), jnp.sum(hg * preact, axis=-1)], axis=-1) / D
    sums = lax.psum_scatter(sums.reshape(-1, slots, 2), "row", scatter_dimension=0, tiled=True)
    weighted = jnp.einsum(
        "ts,si,tsh->tih",
        inv_std,
        onehot,
        hg.reshape(-1, slots, hg.shape[-1]),
        precision=lax.Precision.HIGHEST,
    ).astype(jnp.bfloat16)
    grad = jnp.einsum(
        "th,dh->td",
        weighted.reshape(-1, hg.shape[-1]),
        up_weight,
        preferred_element_type=jnp.float32,
    )
    grad = lax.psum_scatter(
        grad.reshape(-1, image_count, width_local), "row", scatter_dimension=0, tiled=True
    )
    own_normed = lax.dynamic_slice_in_dim(normed, row_index * part, part)
    own_inv = lax.dynamic_slice_in_dim(inv_std, row_index * part, part)
    rest = own_cot.astype(jnp.float32) - own_inv[..., None] * (
        sums[..., 0][..., None] + own_normed * sums[..., 1][..., None]
    )
    total = grad * gain + jnp.einsum("si,tsd->tid", onehot, rest, precision=lax.Precision.HIGHEST)
    total = total / counts[None, :, None]
    return lax.all_gather(total, "noise", axis=0, tiled=True)


def solution(mesh):
    placed = (
        P("row", None, "col"),
        P("col"),
        P("col", "row"),
        P("row", "col"),
        P("row", "noise", "col"),
        P("noise"),
        P(),
    )
    return jax.shard_map(
        body, mesh=mesh, in_specs=placed, out_specs=P("row", None, "col"), check_vma=False
    )
```

profile of v0, /device:TPU:2, one launch (start us, length us, event | category | flops | bytes accessed | tf_op | source)
XLA Modules:
  0.0 281.2 jit_solution(14509511110187522334)
XLA Ops:
  6.5 0.0 copy-start
  6.5 0.0 all-gather.2.cloned.1.call-start
  6.5 19.1 %all_to_all.18 = bf16[16,2,3072]{2,1,0:T(2,128)(2,1)S(1)} all-to-all(bf16[16,2,3072]{2,1,0:T(2,128)(2,1)} %param.11), channel_id=1, replica_groups=mesh['noise'=8,'row'=16,'col'=2] {'noise'}, dimensions={0} | all-to-all | bytes 393216 | tf_op jit(solution)/shard_map/all_to_all | solution.py:42
  25.6 0.1 copy.26
  25.7 0.8 all_to_all.16
  26.5 0.0 all-gather.2.cloned.1.call-update
  26.5 0.0 all-reduce.10.cloned.1.call-start
  26.6 0.1 add_multiply_fusion.1
  26.7 0.1 mul.175
  26.8 1.3 dynamic-slice
  28.8 0.9 dynamic-update-slice
  29.7 10.1 %all-reduce = s32[16]{0:T(128)S(1)} all-reduce(s32[16]{0:T(128)S(1)} %dynamic-update-slice), channel_id=1, replica_groups=mesh['noise'=8,'row'=16,'col'=2] {'noise'}, use_global_device_ids=true, to_apply=%add | all-reduce | flops 16 | bytes 128
  39.8 0.0 copy-done
  39.8 25.4 %all_gather.12 = bf16[32,4,3072]{2,1,0:T(4,128)(2,1)S(1)} all-gather(bf16[2,4,3072]{2,1,0:T(4,128)(2,1)S(1)} %constant_dynamic-slice_fusion.1), channel_id=1, replica_groups=mesh['noise'=8,'row'=16,'col'=2] {'row'}, dimensions={0}, use_global_device_ids=true | all-gather | bytes 835584 | tf_op jit(solution)/shard_map/all_gather | solution.py:44
  65.2 0.1 add_multiply_fusion
  65.3 5.3 %fusion.44 = (f32[32,16]{1,0:T(8,128)S(1)}, f32[32,16,3072]{2,1,0:T(8,128)}) fusion(s32[16]{0:T(128)S(1)} %broadcast_multiply_fusion.1, s32[32,3072]{1,0:T(8,128)S(1)} %add_multiply_fusion, bf16[32,4,3072]{2,1,0:T(4,128)(2,1)S(1)} %all_gather.12, s32[16]{0:T(128)} %bitcast.49), kind=kOutput, calls=%fused_computation.68 | convolution fusion | flops 31456960 | bytes 7473280 | tf_op jit(solution)/shard_map/si,tid->tsd/dot_general | solution.py:49
  70.7 0.0 copy-start.2
  70.7 3.5 %psum.35 = f32[32,16]{1,0:T(8,128)S(1)} all-reduce(f32[32,16]{1,0:T(8,128)S(1)} %get-tuple-element.18), channel_id=1, replica_groups=mesh['noise'=8,'row'=16,'col'=2] {'col'}, use_global_device_ids=true, to_apply=%region_1.0 | all-reduce | flops 512 | bytes 4096 | tf_op jit(solution)/shard_map/psum | solution.py:62
  74.1 3.5 %multiply_reduce_fusion.1 = f32[32,16]{1,0:T(8,128)S(1)} fusion(f32[32,16,3072]{2,1,0:T(8,128)} %get-tuple-element.19, f32[32,16]{1,0:T(8,128)S(1)} %broadcast_multiply_fusion), kind=kLoop, calls=%fused_computation.10 | loop fusion | flops 4718080 | bytes 6295552 | tf_op jit(solution)/shard_map/reduce_sum | solution.py:64
  77.7 0.0 copy-done.2
  77.7 0.0 slice-start
  77.7 3.4 %multiply_reduce_fusion = f32[768]{0:T(1024)S(1)} fusion(bf16[3072,768]{1,0:T(8,128)(2,1)} %param.9, f32[3072]{0:T(1024)S(1)} %copy-done.2), kind=kLoop, calls=%fused_computation.2 | loop fusion | flops 7077120 | bytes 4733952 | tf_op jit(solution)/shard_map/reduce_sum | solution.py:78
  81.1 3.6 %all-reduce.3 = (f32[32,16]{1,0:T(8,128)S(1)}, f32[768]{0:T(1024)S(1)}) all-reduce(f32[32,16]{1,0:T(8,128)S(1)} %multiply_reduce_fusion.1, f32[768]{0:T(1024)S(1)} %multiply_reduce_fusion), channel_id=1, replica_groups=mesh['noise'=8,'row'=16,'col'=2] {'col'}, use_global_device_ids=true, to_apply=%region_3.0 | all-reduce | flops 1280 | bytes 10240 | tf_op jit(solution)/shard_map/psum | solution.py:64
  84.7 0.0 slice-start.1
  84.7 7.3 %multiply_convert_fusion = (bf16[32,16,3072]{2,1,0:T(8,128)(2,1)S(1)}, f32[32,16,3072]{2,1,0:T(8,128)}) fusion(f32[3072]{0:T(1024)S(1)} %copy-done.2, f32[32,16]{1,0:T(8,128)S(1)} %get-tuple-element.17, f32[32,16,3072]{2,1,0:T(8,128)} %get-tuple-element.19, f32[32,16]{1,0:T(8,128)S(1)} %broadcast_multiply_fusion), kind=kLoop, calls=%fused_computation.9 | loop fusion | flops 6291456 | bytes 15745024 | tf_op jit(solution)/shard_map/convert_element_type | solution.py:67
  92.0 0.0 slice-done
  92.0 0.0 slice-done.1
  92.0 3.8 %fusion.46 = f32[512,768]{1,0:T(8,128)} fusion(bf16[512,3072]{1,0:T(8,128)(2,1)S(1)} %bitcast.46, bf16[3072,768]{1,0:T(8,128)(2,1)S(1)} %bitcast.44), kind=kOutput, calls=%fused_computation.70 | convolution fusion | flops 2415919104 | bytes 9437184 | tf_op jit(solution)/shard_map/dot_general | solution.py:69
  95.8 0.0 all-gather.2.cloned.1.call-done
  95.8 0.0 copy-start.3
  95.8 7.1 %fusion.45 = f32[512,768]{1,0:T(8,128)} fusion(bf16[512,3072]{1,0:T(8,128)(2,1)} %bitcast.53, bf16[768,3072]{1,0:T(8,128)(2,1)} %param.10), kind=kOutput, calls=%fused_computation.69 | convolution fusion | flops 2415919104 | bytes 9437184 | tf_op jit(solution)/shard_map/td,hd->th/dot_general | solution.py:72
  102.9 0.0 all-reduce.10.cloned.1.call-update
  102.9 0.2 all-reduce.8.cloned.1.call-start
  103.2 0.0 copy-done.3
  103.2 31.5 %all-reduce.10.cloned.1.call-done = (f32[512,768]{1,0:T(8,128)}, f32[512,768]{1,0:T(8,128)}) async-done(((f32[512,768]{1,0:T(8,128)}, f32[512,768]{1,0:T(8,128)}), (f32[512,768]{1,0:T(8,128)}, f32[512,768]{1,0:T(8,128)})) %all-reduce.10.cloned.1.call-update) | async-done | bytes 3145744 | tf_op jit(solution)/shard_map/psum | solution.py:79
  134.7 3.2 %fusion.10 = (f32[512]{0:T(512)S(1)}, f32[512]{0:T(512)S(1)}, bf16[512,768]{1,0:T(8,128)(2,1)S(1)}) fusion(f32[768]{0:T(1024)S(1)} %get-tuple-element.8, f32[512,768]{1,0:T(8,128)} %get-tuple-element.10, f32[512,768]{1,0:T(8,128)} %get-tuple-element.9), kind=kLoop, calls=%fused_computation.21 | loop fusion | flops 9436160 | bytes 3939328 | tf_op jit(solution)/shard_map/reduce_sum | solution.py:82
  137.9 0.5 convolution_convert_fusion
  138.3 0.0 copy-start.4
  138.4 0.0 copy-start.1
  138.4 4.0 %fusion.6 = f32[32,4,3072]{2,0,1:T(8,128)S(1)} fusion(bf16[3072,768]{1,0:T(8,128)(2,1)} %param.9, bf16[32,4,768]{2,1,0:T(4,128)(2,1)S(1)} %convolution_convert_fusion), kind=kOutput, calls=%fused_computation.12 | convolution fusion | flops 603979776 | bytes 6488064 | tf_op jit(solution)/shard_map/th,dh->td/dot_general | solution.py:91
  142.4 2.2 copy.20
  144.6 0.0 all-reduce.8.cloned.1.call-update
  144.7 0.0 copy-done.4
  144.7 0.6 dynamic-slice.1
  145.9 0.1 fusion.35
  146.1 0.1 stack.10
  146.1 0.1 stack.9
  146.2 69.6 %all-reduce.2 = f32[32,16,2]{1,0,2:T(8,128)S(1)} all-reduce(f32[32,16,2]{1,0,2:T(8,128)S(1)} %maximum_multiply_fusion), channel_id=3, replica_groups=mesh['noise'=8,'row'=16,'col'=2] {'row'}, use_global_device_ids=true, to_apply=%region_11.0.clone | all-reduce | flops 1024 | bytes 8192
  215.9 28.8 %all-reduce.8.cloned.1.call-done = f32[32,4,3072]{2,1,0:T(4,128)} async-done(((f32[32,4,3072]{2,1,0:T(4,128)}), f32[32,4,3072]{2,1,0:T(4,128)}) %all-reduce.8.cloned.1.call-update) | async-done | bytes 1572880
  244.7 0.0 copy-done.1
  244.7 1.4 fusion.9
  246.1 27.8 %all_gather.15 = f32[16,4,3072]{2,1,0:T(4,128)S(1)} all-gather(f32[2,4,3072]{2,1,0:T(4,128)S(1)} %fusion.9), channel_id=1, replica_groups=mesh['noise'=8,'row'=16,'col'=2] {'noise'}, dimensions={0}, use_global_device_ids=true | all-gather | bytes 884736 | tf_op jit(solution)/shard_map/all_gather | solution.py:107
  273.8 0.9 copy.32
  (12 shorter events, 0.1 us)
Async XLA Ops:
  6.5 33.3 %copy-start = (bf16[16,4,3072]{2,1,0:T(4,128)(2,1)S(1)}, bf16[16,4,3072]{2,1,0:T(4,128)(2,1)}, u32[]{:S(2)}) copy-start(bf16[16,4,3072]{2,1,0:T(4,128)(2,1)} %param.7) | copy-start | bytes 1179652
  6.5 89.3 %all-gather.2.cloned.1.call-start = ((), (), s32[]{:S(2)}) async-start(), calls=%async_computation.1 | async-start | bytes 3342336 | tf_op jit(solution)/shard_map/all_gather | solution.py:45
  26.5 108.2 %all-reduce.10.cloned.1.call-start = ((), (), s32[]{:S(2)}) async-start(), calls=%async_computation.3 | async-start | bytes 6291456 | tf_op jit(solution)/shard_map/psum | solution.py:79
  70.7 7.0 %copy-start.2 = (f32[3072]{0:T(1024)S(1)}, f32[3072]{0:T(1024)}, u32[]{:S(2)}) copy-start(f32[3072]{0:T(1024)} %param.8) | copy-start | bytes 36868
  77.7 14.3 %slice-start = ((s8[4718592]{0:T(1024)(128)(4,1)}), s8[524288]{0:T(1024)(128)(4,1)S(1)}, s32[]{:S(2)}) async-start(s8[4718592]{0:T(1024)(128)(4,1)} %bitcast.43), calls=%async_computation.4 | async-start | bytes 1048576
  84.7 7.3 %slice-start.1 = ((s8[4718592]{0:T(1024)(128)(4,1)}), s8[4194304]{0:T(1024)(128)(4,1)S(1)}, s32[]{:S(2)}) async-start(s8[4718592]{0:T(1024)(128)(4,1)} %bitcast.43), calls=%async_computation.5 | async-start | bytes 8388608
  95.8 7.3 %copy-start.3 = (s32[16,1]{0,1:T(1,128)S(1)}, s32[16,1]{0,1:T(1,128)}, u32[]{:S(2)}) copy-start(s32[16,1]{0,1:T(1,128)} %param.13) | copy-start | bytes 196
  102.9 141.7 %all-reduce.8.cloned.1.call-start = ((), (), s32[]{:S(2)}) async-start(), calls=%async_computation.2 | async-start | bytes 3145728
  138.3 6.3 %copy-start.4 = (u32[256]{0:T(256)S(1)}, u32[256]{0:T(256)}, u32[]{:S(2)}) copy-start(u32[256]{0:T(256)} %constant.75) | copy-start | bytes 3076
  138.4 106.3 %copy-start.1 = (bf16[2,16,3072]{2,1,0:T(8,128)(2,1)S(1)}, bf16[2,16,3072]{2,1,0:T(8,128)(2,1)}, u32[]{:S(2)}) copy-start(bf16[2,16,3072]{2,1,0:T(8,128)(2,1)} %all_to_all.16) | copy-start | bytes 589828
Sparse Core Ops, SparseCore 0:
  26.6 49.4 all-gather.1
  103.0 31.6 all-reduce.9
  144.8 99.8 all-reduce.7
where the time goes:
time: 282 us; the launch traced here: 281 us
  blocking collectives  159 us (56%)
  waiting for transfers between devices  60.4 us (21%)
  matrix products  22.1 us (8%)
  other arithmetic  17.7 us (6%)
  between operations  14.6 us (5%)
  local copies, waits for them, and re-layouts  7.19 us (3%)
    unnamed x2, blocking collectives  79.7 us
    psum x1, waiting for transfers between devices, body(): preact, back_grad, ug = lax.psum((preact_part, back_part, ug_part), 'col')  31.5 us
    unnamed x4, waiting for transfers between devices  28.8 us
    all_gather x1, blocking collectives, body(): return lax.all_gather(total, 'noise', axis=0, tiled=True)  27.8 us
    all_gather x1, blocking collectives, body(): plane_images = lax.all_gather(own_images, 'row', axis=0, tiled=True)  25.4 us
    all_to_all x1, blocking collectives, body(): lax.all_to_all(cotangent, 'noise', split_axis=0, concat_axis=1, tiled=True)  19.1 us
    convert_element_type x1, other arithmetic, body(): scaled = (normed * gain).astype(jnp.bfloat16)  7.28 us
    dot_general x1, matrix products, body(): jnp.einsum('td,hd->th', plane_cot.reshape(n, width_local), down_weight, p...  7.09 us
  transfers between devices with their start and end apart: 3, of which 2 were waited for; matrix products, arithmetic and copies ran while one was open for 10% of the time, Pallas kernels for 0%

commit v1 on v0

--- a/solution.py
+++ b/solution.py
@@ -3,6 +3,7 @@
 import jax.numpy as jnp
 from jax import lax
 from jax.sharding import PartitionSpec as P
+from jax.lax import all_gather
 
 D = 6144
 noise_scale = 0.6
@@ -41,8 +42,13 @@
     slots = all_seeds.shape[0]
     own_cot = lax.all_to_all(cotangent, "noise", split_axis=0, concat_axis=1, tiled=True)
     own_images = lax.dynamic_slice_in_dim(images, noise_index * part, part)
-    plane_images = lax.all_gather(own_images, "row", axis=0, tiled=True)
-    plane_cot = lax.all_gather(own_cot, "row", axis=0, tiled=True)
+    plane_images, plane_cot = jnp.split(
+        all_gather(
+            jnp.concatenate([own_images, own_cot], axis=1), axis_name="row", axis=0, tiled=True
+        ),
+        [own_images.shape[1]],
+        axis=1,
+    )
     image_ids = jnp.arange(image_count, dtype=jnp.int32)
     onehot = (assign[:, 0][:, None] == image_ids[None, :]).astype(jnp.float32)
     counts = jnp.sum(onehot, axis=0)

time: 282 us -> 297 us (1.053)
  waiting for transfers between devices: 60.4 us -> 112 us
  blocking collectives: 159 us -> 115 us
  starting transfers between devices: 0.27 us -> 8.72 us
    all_gather x1, waiting for transfers between devices: 0.01 us -> 38.7 us  [body(): all_gather(jnp.concatenate([own_images, own_cot], axis=1), axis_name='row...]
    all_gather x1 -> x0, blocking collectives: 25.4 us -> none  [body(): plane_images = lax.all_gather(own_images, 'row', axis=0, tiled=True)]
    all_to_all x1 -> x0, blocking collectives: 19.1 us -> none  [body(): lax.all_to_all(cotangent, 'noise', split_axis=0, concat_axis=1, tiled=True)]
    all_to_all x0 -> x1, waiting for transfers between devices: none -> 10.4 us  [body(): lax.all_to_all(cotangent, 'noise', split_axis=0, concat_axis=1, tiled=True)]
    all_to_all x0 -> x1, starting transfers between devices: none -> 8.6 us  [body(): lax.all_to_all(cotangent, 'noise', split_axis=0, concat_axis=1, tiled=True)]
    dot_general x1, matrix products: 7.09 us -> 3.79 us  [body(): jnp.einsum('td,hd->th', plane_cot.reshape(n, width_local), down_weight, p...]
  transfers between devices with their start and end apart: 3 -> 4, of which waited for: 2 -> 4; matrix products, arithmetic and copies ran while one was open for 10% -> 2% of each run, Pallas kernels for 0% -> 0%
where the time goes in v1:
time: 297 us
  blocking collectives  115 us (39%)
  waiting for transfers between devices  112 us (38%)
  matrix products  20.2 us (7%)
  other arithmetic  18.9 us (6%)
  between operations  14.7 us (5%)
  starting transfers between devices  8.72 us (3%)
  local copies, waits for them, and re-layouts  7.85 us (3%)
    unnamed x2, blocking collectives  79.7 us
    all_gather x1, waiting for transfers between devices, body(): all_gather(jnp.concatenate([own_images, own_cot], axis=1), axis_name='row...  38.7 us
    psum x1, waiting for transfers between devices, body(): preact, back_grad, ug = lax.psum((preact_part, back_part, ug_part), 'col')  33.9 us
    unnamed x4, waiting for transfers between devices  29 us
    all_gather x1, blocking collectives, body(): return lax.all_gather(total, 'noise', axis=0, tiled=True)  27.8 us
    all_to_all x1, waiting for transfers between devices, body(): lax.all_to_all(cotangent, 'noise', split_axis=0, concat_axis=1, tiled=True)  10.4 us
    all_to_all x1, starting transfers between devices, body(): lax.all_to_all(cotangent, 'noise', split_axis=0, concat_axis=1, tiled=True)  8.6 us
    convert_element_type x1, other arithmetic, body(): scaled = (normed * gain).astype(jnp.bfloat16)  7.68 us
  transfers between devices with their start and end apart: 4, of which 4 were waited for; matrix products, arithmetic and copies ran while one was open for 2% of the time, Pallas kernels for 0%

profile of v1, /device:TPU:2, one launch (start us, length us, event | category | flops | bytes accessed | tf_op | source)
XLA Modules:
  0.0 297.0 jit_solution(16835909474732585543)
XLA Ops:
  6.5 0.0 copy-start
  6.5 0.0 copy-start.2
  6.5 8.6 %all-to-all-start = ((bf16[16,2,3072]{2,1,0:T(2,128)(2,1)}), bf16[16,2,3072]{2,1,0:T(2,128)(2,1)S(1)}, u32[]{:S(2)}, u32[]{:S(2)}) async-start(bf16[16,2,3072]{2,1,0:T(2,128)(2,1)} %param.11), calls=%async_computation | async-start | bytes 393216 | tf_op jit(solution)/shard_map/all_to_all | solution.py:43
  15.1 0.0 all-gather.2.cloned.1.call-start
  15.2 0.0 copy-done
  15.2 10.4 %all-to-all-done = bf16[16,2,3072]{2,1,0:T(2,128)(2,1)S(1)} async-done(((bf16[16,2,3072]{2,1,0:T(2,128)(2,1)}), bf16[16,2,3072]{2,1,0:T(2,128)(2,1)S(1)}, u32[]{:S(2)}, u32[]{:S(2)}) %all-to-all-start) | async-done | bytes 196640 | tf_op jit(solution)/shard_map/all_to_all | solution.py:43
  25.6 0.1 copy.26
  25.8 0.1 all_to_all.16
  25.8 0.8 pad_maximum_fusion
  26.6 0.0 all-gather.2.cloned.1.call-update
  26.7 0.0 all-reduce.10.cloned.1.call-start
  26.7 0.1 add_multiply_fusion.1
  26.8 0.1 mul.175
  26.9 1.3 dynamic-slice
  28.9 0.9 dynamic-update-slice
  29.8 10.1 %all-reduce = s32[16]{0:T(128)S(1)} all-reduce(s32[16]{0:T(128)S(1)} %dynamic-update-slice), channel_id=1, replica_groups=mesh['noise'=8,'row'=16,'col'=2] {'noise'}, use_global_device_ids=true, to_apply=%add | all-reduce | flops 16 | bytes 128
  39.9 3.4 %multiply_reduce_fusion = f32[768]{0:T(1024)S(1)} fusion(bf16[3072,768]{1,0:T(8,128)(2,1)} %param.9, f32[3072]{0:T(1024)} %param.8), kind=kLoop, calls=%fused_computation.2 | loop fusion | flops 7077120 | bytes 4733952 | tf_op jit(solution)/shard_map/reduce_sum | solution.py:84
  43.3 0.1 add_multiply_fusion
  43.4 38.7 %all-gather.2.cloned.1.call-done = bf16[32,20,3072]{2,1,0:T(8,128)(2,1)} async-done(((bf16[2,20,3072]{2,1,0:T(8,128)(2,1)}), bf16[32,20,3072]{2,1,0:T(8,128)(2,1)}) %all-gather.2.cloned.1.call-update) | async-done | bytes 3932176 | tf_op jit(solution)/shard_map/all_gather | solution.py:46
  82.2 0.0 copy-done.2
  82.2 6.8 %fusion.45 = (f32[32,16]{1,0:T(8,128)S(1)}, f32[32,16,3072]{2,1,0:T(8,128)}) fusion(s32[16]{0:T(128)S(1)} %broadcast_multiply_fusion.1, s32[32,3072]{1,0:T(8,128)S(1)} %add_multiply_fusion, s32[16]{0:T(128)S(1)} %bitcast.51, bf16[32,20,3072]{2,1,0:T(8,128)(2,1)} %all-gather.2.cloned.1.call-done), kind=kOutput, calls=%fused_computation.70 | convolution fusion | flops 31456960 | bytes 7473280 | tf_op jit(solution)/shard_map/si,tid->tsd/dot_general | solution.py:55
  89.0 0.0 copy-start.1
  89.0 3.5 %psum.35 = f32[32,16]{1,0:T(8,128)S(1)} all-reduce(f32[32,16]{1,0:T(8,128)S(1)} %get-tuple-element.18), channel_id=1, replica_groups=mesh['noise'=8,'row'=16,'col'=2] {'col'}, use_global_device_ids=true, to_apply=%region_1.0 | all-reduce | flops 512 | bytes 4096 | tf_op jit(solution)/shard_map/psum | solution.py:68
  92.5 0.0 slice-start
  92.5 3.6 %multiply_reduce_fusion.1 = f32[32,16]{1,0:T(8,128)S(1)} fusion(f32[32,16,3072]{2,1,0:T(8,128)} %get-tuple-element.19, f32[32,16]{1,0:T(8,128)S(1)} %broadcast_multiply_fusion), kind=kLoop, calls=%fused_computation.10 | loop fusion | flops 4718080 | bytes 6295552 | tf_op jit(solution)/shard_map/reduce_sum | solution.py:70
  96.1 3.7 %all-reduce.3 = (f32[32,16]{1,0:T(8,128)S(1)}, f32[768]{0:T(1024)S(1)}) all-reduce(f32[32,16]{1,0:T(8,128)S(1)} %multiply_reduce_fusion.1, f32[768]{0:T(1024)S(1)} %multiply_reduce_fusion), channel_id=1, replica_groups=mesh['noise'=8,'row'=16,'col'=2] {'col'}, use_global_device_ids=true, to_apply=%region_3.0 | all-reduce | flops 1280 | bytes 10240 | tf_op jit(solution)/shard_map/psum | solution.py:70
  99.8 0.0 copy-done.1
  99.8 0.0 slice-start.1
  99.8 0.0 slice-start.2
  99.8 0.0 slice-start.4
  99.9 7.7 %multiply_convert_fusion = (bf16[32,16,3072]{2,1,0:T(8,128)(2,1)S(1)}, f32[32,16,3072]{2,1,0:T(8,128)}) fusion(f32[3072]{0:T(1024)S(1)} %copy-done.1, f32[32,16]{1,0:T(8,128)S(1)} %get-tuple-element.17, f32[32,16,3072]{2,1,0:T(8,128)} %get-tuple-element.19, f32[32,16]{1,0:T(8,128)S(1)} %broadcast_multiply_fusion), kind=kLoop, calls=%fused_computation.9 | loop fusion | flops 6291456 | bytes 15745024 | tf_op jit(solution)/shard_map/convert_element_type | solution.py:73
  107.5 0.0 slice-done
  107.5 0.0 slice-done.1
  107.5 0.0 slice-start.3
  107.5 0.0 slice-start.5
  107.6 3.8 %fusion.47 = f32[512,768]{1,0:T(8,128)} fusion(bf16[512,3072]{1,0:T(8,128)(2,1)S(1)} %bitcast.46, bf16[3072,768]{1,0:T(8,128)(2,1)S(1)} %bitcast.43), kind=kOutput, calls=%fused_computation.72 | convolution fusion | flops 2415919104 | bytes 9437184 | tf_op jit(solution)/shard_map/dot_general | solution.py:75
  111.3 0.0 slice-done.2
  111.3 0.0 slice-done.3
  111.3 1.4 split.9
  112.7 0.0 slice-done.4
  112.7 0.0 slice-done.5
  112.7 3.8 %fusion.46 = f32[512,768]{1,0:T(8,128)} fusion(bf16[512,3072]{1,0:T(8,128)(2,1)S(1)} %bitcast.44, bf16[768,3072]{1,0:T(8,128)(2,1)S(1)} %bitcast.56), kind=kOutput, calls=%fused_computation.71 | convolution fusion | flops 2415919104 | bytes 9437184 | tf_op jit(solution)/shard_map/td,hd->th/dot_general | solution.py:78
  116.5 0.0 all-reduce.10.cloned.1.call-update
  116.6 0.0 all-reduce.8.cloned.1.call-start
  116.6 33.9 %all-reduce.10.cloned.1.call-done = (f32[512,768]{1,0:T(8,128)}, f32[512,768]{1,0:T(8,128)}) async-done(((f32[512,768]{1,0:T(8,128)}, f32[512,768]{1,0:T(8,128)}), (f32[512,768]{1,0:T(8,128)}, f32[512,768]{1,0:T(8,128)})) %all-reduce.10.cloned.1.call-update) | async-done | bytes 3145744 | tf_op jit(solution)/shard_map/psum | solution.py:85
  150.5 3.2 %fusion.10 = (f32[512]{0:T(512)S(1)}, f32[512]{0:T(512)S(1)}, bf16[512,768]{1,0:T(8,128)(2,1)S(1)}) fusion(f32[768]{0:T(1024)S(1)} %get-tuple-element.8, f32[512,768]{1,0:T(8,128)} %get-tuple-element.10, f32[512,768]{1,0:T(8,128)} %get-tuple-element.9), kind=kLoop, calls=%fused_computation.21 | loop fusion | flops 9436160 | bytes 3939328 | tf_op jit(solution)/shard_map/reduce_sum | solution.py:88
  153.7 0.5 convolution_convert_fusion
  154.1 0.0 copy-start.3
  154.1 4.0 %fusion.6 = f32[32,4,3072]{2,0,1:T(8,128)S(1)} fusion(bf16[3072,768]{1,0:T(8,128)(2,1)} %param.9, bf16[32,4,768]{2,1,0:T(4,128)(2,1)S(1)} %convolution_convert_fusion), kind=kOutput, calls=%fused_computation.12 | convolution fusion | flops 603979776 | bytes 6488064 | tf_op jit(solution)/shard_map/th,dh->td/dot_general | solution.py:97
  158.1 2.2 copy.20
  160.4 0.0 all-reduce.8.cloned.1.call-update
  160.4 0.0 copy-done.3
  160.4 0.6 dynamic-slice.1
  161.6 0.1 fusion.36
  161.8 0.1 stack.9
  161.8 0.1 stack.10
  161.9 69.5 %all-reduce.2 = f32[32,16,2]{1,0,2:T(8,128)S(1)} all-reduce(f32[32,16,2]{1,0,2:T(8,128)S(1)} %maximum_multiply_fusion), channel_id=3, replica_groups=mesh['noise'=8,'row'=16,'col'=2] {'row'}, use_global_device_ids=true, to_apply=%region_11.0.clone | all-reduce | flops 1024 | bytes 8192
  231.5 29.0 %all-reduce.8.cloned.1.call-done = f32[32,4,3072]{2,1,0:T(4,128)} async-done(((f32[32,4,3072]{2,1,0:T(4,128)}), f32[32,4,3072]{2,1,0:T(4,128)}) %all-reduce.8.cloned.1.call-update) | async-done | bytes 1572880
  260.4 1.4 fusion.9
  261.8 27.8 %all_gather.11 = f32[16,4,3072]{2,1,0:T(4,128)S(1)} all-gather(f32[2,4,3072]{2,1,0:T(4,128)S(1)} %fusion.9), channel_id=1, replica_groups=mesh['noise'=8,'row'=16,'col'=2] {'noise'}, dimensions={0}, use_global_device_ids=true | all-gather | bytes 884736 | tf_op jit(solution)/shard_map/all_gather | solution.py:113
  289.6 0.9 copy.32
  (14 shorter events, 0.1 us)
Async XLA Ops:
  6.5 8.7 %copy-start = (bf16[16,4,3072]{2,1,0:T(4,128)(2,1)S(1)}, bf16[16,4,3072]{2,1,0:T(4,128)(2,1)}, u32[]{:S(2)}) copy-start(bf16[16,4,3072]{2,1,0:T(4,128)(2,1)} %param.7) | copy-start | bytes 1179652
  6.5 75.6 %copy-start.2 = (s32[16,1]{0,1:T(1,128)S(1)}, s32[16,1]{0,1:T(1,128)}, u32[]{:S(2)}) copy-start(s32[16,1]{0,1:T(1,128)} %param.13) | copy-start | bytes 196
  6.5 19.1 %all-to-all-start = ((bf16[16,2,3072]{2,1,0:T(2,128)(2,1)}), bf16[16,2,3072]{2,1,0:T(2,128)(2,1)S(1)}, u32[]{:S(2)}, u32[]{:S(2)}) async-start(bf16[16,2,3072]{2,1,0:T(2,128)(2,1)} %param.11), calls=%async_computation | async-start | bytes 393216 | tf_op jit(solution)/shard_map/all_to_all | solution.py:43
  15.1 67.0 %all-gather.2.cloned.1.call-start = ((), (), s32[]{:S(2)}) async-start(), calls=%async_computation.1 | async-start | bytes 5013504 | tf_op jit(solution)/shard_map/all_gather | solution.py:46
  26.7 123.8 %all-reduce.10.cloned.1.call-start = ((), (), s32[]{:S(2)}) async-start(), calls=%async_computation.3 | async-start | bytes 6291456 | tf_op jit(solution)/shard_map/psum | solution.py:85
  89.0 10.8 %copy-start.1 = (f32[3072]{0:T(1024)S(1)}, f32[3072]{0:T(1024)}, u32[]{:S(2)}) copy-start(f32[3072]{0:T(1024)} %param.8) | copy-start | bytes 36868
  92.5 15.1 %slice-start = ((s8[4718592]{0:T(1024)(128)(4,1)}), s8[524288]{0:T(1024)(128)(4,1)S(1)}, s32[]{:S(2)}) async-start(s8[4718592]{0:T(1024)(128)(4,1)} %bitcast.42), calls=%async_computation.4 | async-start | bytes 1048576
  99.8 7.7 %slice-start.1 = ((s8[4718592]{0:T(1024)(128)(4,1)}), s8[4194304]{0:T(1024)(128)(4,1)S(1)}, s32[]{:S(2)}) async-start(s8[4718592]{0:T(1024)(128)(4,1)} %bitcast.42), calls=%async_computation.5 | async-start | bytes 8388608
  99.8 11.5 %slice-start.2 = ((s8[4718592]{0:T(1024)(128)(4,1)}), s8[4194304]{0:T(1024)(128)(4,1)S(1)}, s32[]{:S(2)}) async-start(s8[4718592]{0:T(1024)(128)(4,1)} %bitcast.47), calls=%async_computation.6 | async-start | bytes 8388608
  99.8 12.9 %slice-start.4 = ((s8[4718592]{0:T(1024)(128)(4,1)}), s8[4194304]{0:T(1024)(128)(4,1)S(1)}, s32[]{:S(2)}) async-start(s8[4718592]{0:T(1024)(128)(4,1)} %bitcast.55), calls=%async_computation.8 | async-start | bytes 8388608
  107.5 3.8 %slice-start.3 = ((s8[4718592]{0:T(1024)(128)(4,1)}), s8[524288]{0:T(1024)(128)(4,1)S(1)}, s32[]{:S(2)}) async-start(s8[4718592]{0:T(1024)(128)(4,1)} %bitcast.47), calls=%async_computation.7 | async-start | bytes 1048576
  107.5 5.2 %slice-start.5 = ((s8[4718592]{0:T(1024)(128)(4,1)}), s8[524288]{0:T(1024)(128)(4,1)S(1)}, s32[]{:S(2)}) async-start(s8[4718592]{0:T(1024)(128)(4,1)} %bitcast.55), calls=%async_computation.9 | async-start | bytes 1048576
  116.6 143.9 %all-reduce.8.cloned.1.call-start = ((), (), s32[]{:S(2)}) async-start(), calls=%async_computation.2 | async-start | bytes 3145728
  154.1 6.3 %copy-start.3 = (u32[256]{0:T(256)S(1)}, u32[256]{0:T(256)}, u32[]{:S(2)}) copy-start(u32[256]{0:T(256)} %constant.75) | copy-start | bytes 3076
Sparse Core Ops, SparseCore 0:
  26.8 55.3 all-gather.1
  116.7 33.7 all-reduce.9
  160.5 99.8 all-reduce.7
